TPU v7x, 32 devices: a whole 2x2x4 slice. The times are simulated.
32 devices in a mesh: seq: 8 (over y, x, core), mp: 4 (over z).
Axes of the slice: x: 2, y: 2, z: 4, core: 2. Of those that a mesh axis runs over, the one named last changes fastest.
Arguments:
- qkv: bfloat16 [3, 8192, 8192], P(None, 'mp', 'seq'), may hold values from -6 to 6
- short_taps: bfloat16 [3, 8192, 7], P(None, 'mp'), may hold values from -2 to 2
- medium_taps: bfloat16 [8192, 128], P('mp'), may hold values from -0.5 to 0.5
- skip_gain: float32 [8192], P('mp'), may hold values from -4 to 4
- w_out: bfloat16 [8192, 8192], P('mp'), may hold values from -0.09375 to 0.09375
- resid: bfloat16 [8192, 8192], P('mp', 'seq'), may hold values from -6 to 6
- steer: float32 [8192], P('mp'), may hold values from -5 to 5
Outputs:
- layer_out: bfloat16 [8192, 8192], P('mp', 'seq')
All inputs are finite; a program needn't handle non-finite values.
Results may differ from a plain program's by a relative error of at most 0.017.
Values may be sent and summed in bfloat16 or wider, within the bound.
A program may use at most 192 MiB of HBM per device.

v0:
```python
import jax
import jax.numpy as jnp
from jax import lax
from jax.sharding import PartitionSpec as P

STAPS = 7
MTAPS = 128


def from_behind(value, axis, steps):
    count = lax.axis_size(axis)
    leading, last = (max(0, -steps), min(count, count - steps))
    return lax.ppermute(value, axis, [(source, source + steps) for source in range(leading, last)])


def featurize(padded, taps, length):
    f32 = jnp.float32
    start = padded.shape[2] - length
    wide_taps = taps.astype(f32)
    filtered = jnp.zeros((3, padded.shape[1], length), f32)
    for j in range(STAPS):
        window = padded[:, :, start - j : start - j + length].astype(f32)
        filtered = filtered + wide_taps[:, :, j : j + 1] * window
    kv_half = (filtered[1] * filtered[2]).astype(jnp.bfloat16)
    return (filtered[0], kv_half)


def finish(q_filt, kv_half, before_tile, filt, skip_part):
    count, length = kv_half.shape
    padded = jnp.concatenate([before_tile[:, 1:], kv_half], 1).astype(jnp.float32)
    kernel = jnp.flip(filt.astype(jnp.float32), 1)[:, None, :]
    med = lax.conv_general_dilated(
        padded[None],
        kernel,
        (1,),
        "VALID",
        dimension_numbers=("NCH", "OIH", "NCH"),
        feature_group_count=count,
        precision=lax.Precision.HIGHEST,
    )[0]
    med = med + skip_part[:, None] * kv_half.astype(jnp.float32)
    return (q_filt * med).astype(jnp.bfloat16)


def shards(qkv, short_taps, medium_taps, skip_gain, w_out, resid, steer):
    slab = qkv.shape[2]
    rim = from_behind(qkv[:, :, slab - (STAPS - 1) :], "seq", 1)
    padded = jnp.concatenate([rim, qkv], 2)
    q_filt, kv_half = featurize(padded, short_taps, slab)
    before_tile = from_behind(kv_half[:, slab - MTAPS :], "seq", 1)
    y_slab = finish(q_filt, kv_half, before_tile, medium_taps, skip_gain)
    part = lax.dot_general(
        w_out, y_slab, (((0,), (0,)), ((), ())), preferred_element_type=jnp.float32
    )
    proj = lax.psum_scatter(
        part.astype(jnp.bfloat16).astype(jnp.float32).astype(jnp.bfloat16),
        "mp",
        scatter_dimension=0,
        tiled=True,
    ).astype(jnp.float32)
    return (resid.astype(jnp.float32) + proj + steer[:, None]).astype(jnp.bfloat16)


def solution(mesh):
    return jax.shard_map(
        shards,
        mesh=mesh,
        in_specs=(
            P(None, "mp", "seq"),
            P(None, "mp", None),
            P("mp", None),
            P("mp"),
            P("mp", None),
            P("mp", "seq"),
            P("mp"),
        ),
        out_specs=P("mp", "seq"),
        check_vma=False,
    )
```

profile of v0, /device:TPU:0, one launch (start us, length us, event | category | flops | bytes accessed | tf_op | source)
XLA Modules:
  0.0 675.2 jit_solution(18156092512978954253)
XLA Ops:
  6.5 0.0 copy-start.2
  6.5 0.0 reduce-scatter.2.cloned.1.call-start
  6.5 17.1 %copy.12 = bf16[3,2048,1024]{1,2,0:T(8,128)(2,1)} copy(bf16[3,2048,1024]{2,1,0:T(8,128)(2,1)} %param.7) | data formatting | bytes 25165824 | tf_op args[0]
  23.6 0.9 slice.80
  24.5 2.4 collective-permute-start
  26.9 0.0 copy-done.2
  26.9 0.1 fusion.26
  27.2 0.7 collective-permute-done
  27.8 38.1 %multiply_add_fusion = f32[3,2048,1024]{1,2,0:T(8,128)} fusion(bf16[3,2048,1024]{1,2,0:T(8,128)(2,1)} %copy.12, bf16[3,2048,6]{1,2,0:T(8,128)(2,1)S(1)} %collective-permute-done, f32[3,2048]{1,0:T(4,128)S(1)} %get-tuple-element.12, f32[3,2048]{1,0:T(4,128)S(1)} %get-tuple-element.13, f32[3,2048]{1,0:T(4,128)S(1)} %get-tuple-element.14, ...), kind=kLoop, calls=%fused_computation.5 | loop fusion | flops 239075328 | bytes 37994496 | tf_op jit(solution)/shard_map/add | solution.py:23
  66.0 0.0 copy-start.1
  66.0 6.5 fusion.18
  72.5 0.0 copy-start
  72.5 2.0 copy-done
  74.6 0.9 slice.99
  75.4 5.2 collective-permute-start.1
  80.6 0.0 copy-done.1
  80.7 1.3 rev.4
  82.0 0.8 copy.17
  82.8 0.0 collective-permute-done.1
  82.8 0.1 slice.100
  82.9 3.4 maximum_bitcast_fusion
  86.3 0.7 pad
  87.0 2.6 copy.16
  89.6 0.0 copy-start.5
  89.6 1.3 slice.101
  91.0 1.9 fusion.32
  92.9 0.0 copy-done.5
  92.9 215.3 %broadcast_select_fusion = f32[8,144,2048]{2,0,1:T(8,128)S(1)} fusion(pred[8,144]{0,1:T(8,128)(4,1)S(1)} %copy-done.5, f32[2048,1,128]{0,1,2:T(1,128)S(1)} %copy.17, bf16[2048,8,271]{0,1,2:T(8,128)(2,1)S(1)} %fusion.32), kind=kOutput, calls=%fused_computation.33 | convolution fusion | flops 3626237952 | bytes 19367040 | tf_op jit(solution)/shard_map/conv_general_dilated | solution.py:32
  308.2 0.0 copy-start.4
  308.2 9.1 %copy.18 = f32[8,144,2048]{2,1,0:T(8,128)} copy(f32[8,144,2048]{2,0,1:T(8,128)S(1)} %broadcast_select_fusion) | data formatting | bytes 18874368 | tf_op jit(solution)/shard_map/conv_general_dilated | solution.py:32
  317.3 0.0 copy-done.4
  317.3 46.8 %convert_bitcast_fusion = bf16[8192,1024]{0,1:T(8,128)(2,1)} fusion(bf16[2048,8192]{1,0:T(8,128)(2,1)} %param.11, f32[1,1152,2048]{2,1,0:T(8,128)} %bitcast.53, f32[3,2048,1024]{1,2,0:T(8,128)} %multiply_add_fusion, bf16[2048,1024]{0,1:T(8,128)(2,1)} %copy-done, f32[2048]{0:T(1024)S(1)} %copy-done.4), kind=kOutput, calls=%fused_computation.8 | convolution fusion | flops 34378612736 | bytes 71311360 | tf_op jit(solution)/shard_map/dot_general | solution.py:52
  364.1 0.0 copy-start.3
  364.1 0.0 reduce-scatter.2.cloned.1.call-update
  364.1 6.7 copy.11
  370.8 283.3 %reduce-scatter.2.cloned.1.call-done = bf16[2048,1024]{0,1:T(8,128)(2,1)} async-done(((bf16[8192,1024]{0,1:T(8,128)(2,1)}), bf16[2048,1024]{0,1:T(8,128)(2,1)}) %reduce-scatter.2.cloned.1.call-update) | async-done | bytes 4194320 | tf_op jit(solution)/shard_map/reduce_scatter | solution.py:55
  654.1 0.0 copy-done.3
  654.1 7.8 %add_convert_fusion = bf16[2048,1024]{0,1:T(8,128)(2,1)} fusion(bf16[2048,1024]{0,1:T(8,128)(2,1)} %reduce-scatter.2.cloned.1.call-done, bf16[2048,1024]{0,1:T(8,128)(2,1)} %copy.11, f32[2048]{0:T(1024)S(1)} %copy-done.3), kind=kLoop, calls=%fused_computation.31 | loop fusion | flops 10485760 | bytes 12591104 | tf_op jit(solution)/shard_map/convert_element_type | solution.py:61
  661.9 6.4 copy.19
  (4 shorter events, 0.1 us)
Async XLA Ops:
  6.5 20.4 %copy-start.2 = (bf16[3,2048,7]{1,2,0:T(8,128)(2,1)S(1)}, bf16[3,2048,7]{1,2,0:T(8,128)(2,1)}, u32[]{:S(2)}) copy-start(bf16[3,2048,7]{1,2,0:T(8,128)(2,1)} %param.8) | copy-start | bytes 258052
  6.5 647.6 %reduce-scatter.2.cloned.1.call-start = ((), (), s32[]{:S(2)}) async-start(), calls=%async_computation.1 | async-start | bytes 20971520 | tf_op jit(solution)/shard_map/reduce_scatter | solution.py:55
  24.5 3.3 collective-permute-start
  66.0 14.7 %copy-start.1 = (bf16[2048,128]{1,0:T(8,128)(2,1)S(1)}, bf16[2048,128]{1,0:T(8,128)(2,1)}, u32[]{:S(2)}) copy-start(bf16[2048,128]{1,0:T(8,128)(2,1)} %param.9) | copy-start | bytes 1572868
  72.5 2.0 copy-start
  75.4 7.4 %collective-permute-start.1 = (bf16[2048,128]{0,1:T(8,128)(2,1)}, bf16[2048,128]{0,1:T(8,128)(2,1)S(1)}, u32[]{:S(2)}, u32[]{:S(2)}) collective-permute-start(bf16[2048,128]{0,1:T(8,128)(2,1)} %slice.99), channel_id=1, source_target_pairs={{0,4},{4,8},{8,12},{12,16},{16,20},{20,24},{24,28},{1,5},{5,9},{9,... | collective-permute-start | bytes 1572872 | tf_op jit(solution)/shard_map/ppermute | solution.py:13
  89.6 3.2 copy-start.5
  308.2 9.1 %copy-start.4 = (f32[2048]{0:T(1024)S(1)}, f32[2048]{0:T(1024)}, u32[]{:S(2)}) copy-start(f32[2048]{0:T(1024)} %param.10) | copy-start | bytes 24580
  364.1 290.0 %copy-start.3 = (f32[2048]{0:T(1024)S(1)}, f32[2048]{0:T(1024)}, u32[]{:S(2)}) copy-start(f32[2048]{0:T(1024)} %param.13) | copy-start | bytes 24580
Sparse Core Ops, SparseCore 0:
  364.2 289.8 reduce-scatter.1
where the time goes:
time: 676 us; the launch traced here: 675 us
  waiting for transfers between devices  284 us (42%)
  matrix products  262 us (39%)
  other arithmetic  57.7 us (9%)
  local copies, waits for them, and re-layouts  50.1 us (7%)
  between operations  13.6 us (2%)
  starting transfers between devices  7.59 us (1%)
    reduce_scatter x1, waiting for transfers between devices, shards(): lax.psum_scatter(part.astype(jnp.bfloat16).astype(jnp.float32).astype(jnp...  283 us
    conv_general_dilated x1, matrix products, finish(): lax.conv_general_dilated(padded[None], kernel, (1,), 'VALID', dimension_n...  215 us
    dot_general x1, matrix products, shards(): lax.dot_general(w_out, y_slab, (((0,), (0,)), ((), ())), preferred_elemen...  46.8 us
    add x1, other arithmetic, featurize(): filtered = filtered + wide_taps[:, :, j:j + 1] * window  38.1 us
    unnamed x18, local copies, waits for them, and re-layouts  25.9 us
  transfers between devices with their start and end apart: 3, of which 2 were waited for; matrix products, arithmetic and copies ran while one was open for 1% of the time, Pallas kernels for 0%

commit v1 on v0

v1 whole, which is shorter than its diff:
```python
import jax
import jax.numpy as jnp
from jax import lax
from jax.experimental import pallas as pl
from jax.experimental.pallas import tpu as pltpu
from jax.sharding import PartitionSpec as P

STAPS = 7
MTAPS = 128
WINDOW = 256
LANES = 128
F32 = jnp.float32
BF16 = jnp.bfloat16


def from_behind(value, axis, steps):
    count = lax.axis_size(axis)
    return lax.ppermute(value, axis, [(source, source + steps) for source in range(count - steps)])


def feature_kernel(before_ref, now_ref, short_ref, medium_ref, y_ref, wide, kv):
    for s in range(3):
        wide[s, :WINDOW] = before_ref[s].astype(F32).T
        wide[s, WINDOW:] = now_ref[s].astype(F32).T

    def short(s, row):
        total = short_ref[s, 0:1] * wide[s, row : row + LANES]
        for j in range(1, STAPS):
            total = total + short_ref[s, j : j + 1] * wide[s, row - j : row - j + LANES]
        return total

    for row in range(WINDOW - MTAPS, 2 * WINDOW, LANES):
        place = row - (WINDOW - MTAPS)
        kv[place : place + LANES] = (short(1, row) * short(2, row)).astype(BF16).astype(F32)

    for row in range(0, WINDOW, LANES):
        total = jnp.zeros((LANES, LANES), F32)
        for low in range(8):
            start = row + 8 - low
            block = kv[start : start + LANES + MTAPS - 8]
            for high in range(0, MTAPS, 8):
                first = MTAPS - 8 - high
                total = total + medium_ref[high + low : high + low + 1] * block[first : first + LANES]
        y_ref[:, row : row + LANES] = (short(0, WINDOW + row) * total).T.astype(BF16)


def features(before, before_index, now, now_index, short, medium):
    channels = now.shape[1]
    return pl.pallas_call(
        feature_kernel,
        grid=(channels // LANES,),
        in_specs=[
            pl.BlockSpec((3, LANES, WINDOW), lambda c: (0, c, before_index)),
            pl.BlockSpec((3, LANES, WINDOW), lambda c: (0, c, now_index)),
            pl.BlockSpec((3, STAPS, LANES), lambda c: (0, 0, c)),
            pl.BlockSpec((MTAPS, LANES), lambda c: (0, c)),
        ],
        out_specs=pl.BlockSpec((LANES, WINDOW), lambda c: (c, 0)),
        out_shape=jax.ShapeDtypeStruct((channels, WINDOW), BF16),
        scratch_shapes=[
            pltpu.VMEM((3, 2 * WINDOW, LANES), F32),
            pltpu.VMEM((MTAPS + WINDOW, LANES), F32),
        ],
        cost_estimate=pl.CostEstimate(
            flops=2 * channels * WINDOW * (MTAPS + 4 * STAPS),
            bytes_accessed=14 * channels * WINDOW,
            transcendentals=0,
        ),
    )(before, now, short, medium)


def shards(qkv, short_taps, medium_taps, skip_gain, w_out, resid, steer):
    slab = qkv.shape[2]
    short = jnp.swapaxes(short_taps.astype(F32), 1, 2)
    medium = medium_taps.astype(F32)
    medium = jnp.concatenate([medium[:, :1] + skip_gain[:, None], medium[:, 1:]], 1).T
    rim = from_behind(qkv[:, :, slab - WINDOW :], "seq", 1)
    count = slab // WINDOW
    pieces = [None] * count
    for i in reversed(range(count)):
        before = (rim, 0) if i == 0 else (qkv, i - 1)
        y = features(*before, qkv, i, short, medium)
        part = lax.dot_general(
            w_out, y, (((0,), (0,)), ((), ())), preferred_element_type=F32
        ).astype(BF16)
        proj = lax.psum_scatter(part, "mp", scatter_dimension=0, tiled=True).astype(F32)
        own = resid[:, i * WINDOW : (i + 1) * WINDOW].astype(F32)
        pieces[i] = (own + proj + steer[:, None]).astype(BF16)
    return jnp.concatenate(pieces, 1)


def solution(mesh):
    return jax.shard_map(
        shards,
        mesh=mesh,
        in_specs=(
            P(None, "mp", "seq"),
            P(None, "mp", None),
            P("mp", None),
            P("mp"),
            P("mp", None),
            P("mp", "seq"),
            P("mp"),
        ),
        out_specs=P("mp", "seq"),
        check_vma=False,
    )
```

time: 676 us -> 398 us (0.59)
  matrix products: 262 us -> 68.3 us
  Pallas kernels: 0 us -> 132 us
  waiting for transfers between devices: 284 us -> 152 us
  other arithmetic: 57.7 us -> 8.54 us
  local copies, waits for them, and re-layouts: 50.1 us -> 20.7 us
    conv_general_dilated x1 -> x0, matrix products: 215 us -> none  [finish(): lax.conv_general_dilated(padded[None], kernel, (1,), 'VALID', dimension_n...]
    reduce_scatter x1 -> x4, waiting for transfers between devices: 283 us -> 147 us  [shards(): lax.psum_scatter(part, 'mp', scatter_dimension=0, tiled=True).astype(F32)]
    pallas_call x0 -> x4, Pallas kernels: none -> 132 us  [features(): pl.pallas_call(feature_kernel, grid=(channels // LANES,), in_specs=[pl.Bl...]
    add x1, other arithmetic: 38.1 us -> 0.01 us  [shards(): medium[:, :1] + skip_gain[:, None]]
    dot_general x1 -> x4, matrix products: 46.8 us -> 68.3 us  [shards(): lax.dot_general(w_out, y, (((0,), (0,)), ((), ())), preferred_element_typ...]
    unnamed x18 -> x13, local copies, waits for them, and re-layouts: 25.9 us -> 8.21 us
    conv_general_dilated x3 -> x0, local copies, waits for them, and re-layouts: 13 us -> none  [finish(): lax.conv_general_dilated(padded[None], kernel, (1,), 'VALID', dimension_n...]
    convert_element_type x2, other arithmetic: 14.3 us -> 4.53 us  [the longest x1 4.43 us: shards(): pieces[i] = (own + proj + steer[:, None]).astype(BF16)]
  transfers between devices with their start and end apart: 3 -> 5, of which waited for: 2 -> 3; matrix products, arithmetic and copies ran while one was open for 1% -> 16% of each run, Pallas kernels for 0% -> 25%
where the time goes in v1:
time: 398 us
  waiting for transfers between devices  152 us (38%)
  Pallas kernels  132 us (33%)
  matrix products  68.3 us (17%)
  local copies, waits for them, and re-layouts  20.7 us (5%)
  between operations  13.2 us (3%)
  other arithmetic  8.54 us (2%)
    reduce_scatter x4, waiting for transfers between devices, shards(): lax.psum_scatter(part, 'mp', scatter_dimension=0, tiled=True).astype(F32)  147 us
    pallas_call x4, Pallas kernels, features(): pl.pallas_call(feature_kernel, grid=(channels // LANES,), in_specs=[pl.Bl...  132 us
    dot_general x4, matrix products, shards(): lax.dot_general(w_out, y, (((0,), (0,)), ((), ())), preferred_element_typ...  68.3 us
    unnamed x13, local copies, waits for them, and re-layouts  8.21 us
  transfers between devices with their start and end apart: 5, of which 3 were waited for; matrix products, arithmetic and copies ran while one was open for 16% of the time, Pallas kernels for 25%

profile of v1, /device:TPU:0, one launch (start us, length us, event | category | flops | bytes accessed | tf_op | source)
XLA Modules:
  0.0 397.8 jit_solution(6695833780579802014)
XLA Ops:
  6.5 0.0 copy-start.1
  6.5 0.0 copy-start.2
  6.5 0.0 reduce-scatter.11.cloned.1.call-start
  6.5 1.3 copy.9
  7.8 0.1 convert_element_type.65
  7.9 0.1 slice.29
  8.1 0.0 copy-done.1
  8.1 0.7 convert_bitcast_fusion.short_ref
  8.8 0.0 copy-done.2
  8.8 1.1 maximum_bitcast_fusion.medium_ref
  9.9 33.0 %shard_map.76 = bf16[2048,256]{1,0:T(8,128)(2,1)} custom-call(bf16[3,2048,1024]{2,1,0:T(8,128)(2,1)} %now_ref.7, bf16[3,2048,1024]{2,1,0:T(8,128)(2,1)} %now_ref.7, f32[3,7,2048]{2,1,0:T(8,128)} %convert_bitcast_fusion.short_ref, f32[128,2048]{1,0:T(8,128)} %maximum_bitcast_fusion.medium_ref), custom_call_target="tpu_custom_call" | custom-call | flops 163577856 | bytes 7340032 | tf_op jit(solution)/shard_map/pallas_call | solution.py:49
  42.9 16.8 %fusion.3 = bf16[8192,256]{0,1:T(8,128)(2,1)} fusion(bf16[2048,256]{1,0:T(8,128)(2,1)} %shard_map.76, bf16[2048,8192]{1,0:T(8,128)(2,1)} %param.11), kind=kOutput, calls=%fused_computation.7 | convolution fusion | flops 8592031744 | bytes 38797312 | tf_op jit(solution)/shard_map/dot_general | solution.py:83
  59.7 0.0 reduce-scatter.11.cloned.1.call-update
  59.7 0.2 reduce-scatter.7.cloned.1.call-start
  59.9 33.0 %shard_map.74 = bf16[2048,256]{1,0:T(8,128)(2,1)} custom-call(bf16[3,2048,1024]{2,1,0:T(8,128)(2,1)} %now_ref.7, bf16[3,2048,1024]{2,1,0:T(8,128)(2,1)} %now_ref.7, f32[3,7,2048]{2,1,0:T(8,128)} %convert_bitcast_fusion.short_ref, f32[128,2048]{1,0:T(8,128)} %maximum_bitcast_fusion.medium_ref), custom_call_target="tpu_custom_call" | custom-call | flops 163577856 | bytes 7340032 | tf_op jit(solution)/shard_map/pallas_call | solution.py:49
  92.9 17.0 %fusion.1 = bf16[8192,256]{0,1:T(8,128)(2,1)} fusion(bf16[2048,256]{1,0:T(8,128)(2,1)} %shard_map.74, bf16[2048,8192]{1,0:T(8,128)(2,1)} %param.11), kind=kOutput, calls=%fused_computation.5 | convolution fusion | flops 8592031744 | bytes 38797312 | tf_op jit(solution)/shard_map/dot_general | solution.py:83
  109.9 0.0 reduce-scatter.7.cloned.1.call-update
  110.0 0.3 reduce-scatter.9.cloned.1.call-start
  110.2 33.0 %shard_map.75 = bf16[2048,256]{1,0:T(8,128)(2,1)} custom-call(bf16[3,2048,1024]{2,1,0:T(8,128)(2,1)} %now_ref.7, bf16[3,2048,1024]{2,1,0:T(8,128)(2,1)} %now_ref.7, f32[3,7,2048]{2,1,0:T(8,128)} %convert_bitcast_fusion.short_ref, f32[128,2048]{1,0:T(8,128)} %maximum_bitcast_fusion.medium_ref), custom_call_target="tpu_custom_call" | custom-call | flops 163577856 | bytes 7340032 | tf_op jit(solution)/shard_map/pallas_call | solution.py:49
  143.3 17.5 %fusion.2 = bf16[8192,256]{0,1:T(8,128)(2,1)} fusion(bf16[2048,256]{1,0:T(8,128)(2,1)} %shard_map.75, bf16[2048,8192]{1,0:T(8,128)(2,1)} %param.11), kind=kOutput, calls=%fused_computation.6 | convolution fusion | flops 8592031744 | bytes 38797312 | tf_op jit(solution)/shard_map/dot_general | solution.py:83
  160.8 0.0 reduce-scatter.9.cloned.1.call-update
  160.8 0.0 reduce-scatter.5.cloned.1.call-start
  160.9 2.1 slice.22
  163.0 2.9 collective-permute-start
  165.9 4.8 %collective-permute-done.before_ref = bf16[3,2048,256]{2,1,0:T(8,128)(2,1)S(1)} collective-permute-done((bf16[3,2048,256]{2,1,0:T(8,128)(2,1)S(1)}, bf16[3,2048,256]{2,1,0:T(8,128)(2,1)S(1)}, u32[]{:S(2)}, u32[]{:S(2)}) %collective-permute-start) | collective-permute-done | bytes 3145760 | tf_op jit(solution)/shard_map/ppermute | solution.py:18
  170.7 0.0 copy-start
  170.7 1.7 copy-done
  172.3 33.0 %shard_map.73 = bf16[2048,256]{1,0:T(8,128)(2,1)} custom-call(bf16[3,2048,256]{2,1,0:T(8,128)(2,1)} %copy-done, bf16[3,2048,1024]{2,1,0:T(8,128)(2,1)} %now_ref.7, f32[3,7,2048]{2,1,0:T(8,128)} %convert_bitcast_fusion.short_ref, f32[128,2048]{1,0:T(8,128)} %maximum_bitcast_fusion.medium_ref), custom_call_target="tpu_custom_call" | custom-call | flops 163577856 | bytes 7340032 | tf_op jit(solution)/shard_map/pallas_call | solution.py:49
  205.3 17.0 %fusion = bf16[8192,256]{0,1:T(8,128)(2,1)} fusion(bf16[2048,256]{1,0:T(8,128)(2,1)} %shard_map.73, bf16[2048,8192]{1,0:T(8,128)(2,1)} %param.11), kind=kOutput, calls=%fused_computation.4 | convolution fusion | flops 8592031744 | bytes 38797312 | tf_op jit(solution)/shard_map/dot_general | solution.py:83
  222.3 0.0 reduce-scatter.5.cloned.1.call-update
  222.3 3.8 fusion.4
  226.1 0.0 copy-start.3
  226.1 0.6 copy.14
  226.8 0.6 copy.15
  227.4 1.7 copy.16
  229.1 2.3 copy.17
  231.4 0.0 reduce-scatter.11.cloned.1.call-done
  231.4 0.0 reduce-scatter.7.cloned.1.call-done
  231.4 67.2 %reduce-scatter.9.cloned.1.call-done = bf16[2048,256]{0,1:T(8,128)(2,1)} async-done(((bf16[8192,256]{0,1:T(8,128)(2,1)}), bf16[2048,256]{0,1:T(8,128)(2,1)}) %reduce-scatter.9.cloned.1.call-update) | async-done | bytes 1048592 | tf_op jit(solution)/shard_map/reduce_scatter | solution.py:86
  298.6 79.5 %reduce-scatter.5.cloned.1.call-done = bf16[2048,256]{0,1:T(8,128)(2,1)} async-done(((bf16[8192,256]{0,1:T(8,128)(2,1)}), bf16[2048,256]{0,1:T(8,128)(2,1)}) %reduce-scatter.5.cloned.1.call-update) | async-done | bytes 1048592 | tf_op jit(solution)/shard_map/reduce_scatter | solution.py:86
  378.2 0.0 copy-done.3
  378.2 4.4 %add_convert_fusion.3 = (bf16[2048,256]{0,1:T(8,128)(2,1)S(1)}, bf16[2048,256]{0,1:T(8,128)(2,1)S(1)}, bf16[2048,256]{0,1:T(8,128)(2,1)S(1)}, bf16[2048,256]{0,1:T(8,128)(2,1)S(1)}) fusion(bf16[2048,256]{0,1:T(8,128)(2,1)} %reduce-scatter.5.cloned.1.call-done, bf16[2048,256]{0,1:T(8,128)(2,1)S(1)} %copy.14, f32[2048]{0:T(1024)S(1)} %copy-done.3, ...), kind=kLoop, calls=%fused_computation.12 | loop fusion | flops 10485760 | bytes 12591104 | tf_op jit(solution)/shard_map/convert_element_type | solution.py:88
  382.6 2.2 pad_maximum_fusion
  384.8 6.4 %copy.13 = bf16[2048,1024]{1,0:T(8,128)(2,1)} copy(bf16[2048,1024]{0,1:T(8,128)(2,1)} %pad_maximum_fusion) | data formatting | bytes 8388608 | tf_op jit(solution)/shard_map/concatenate | solution.py:89
  (1 shorter events, 0.0 us)
Async XLA Ops:
  6.5 1.5 copy-start.1
  6.5 2.2 copy-start.2
  6.5 224.9 %reduce-scatter.11.cloned.1.call-start = ((), (), s32[]{:S(2)}) async-start(), calls=%async_computation.7 | async-start | bytes 5242880 | tf_op jit(solution)/shard_map/reduce_scatter | solution.py:86
  59.7 171.7 %reduce-scatter.7.cloned.1.call-start = ((), (), s32[]{:S(2)}) async-start(), calls=%async_computation.5 | async-start | bytes 5242880 | tf_op jit(solution)/shard_map/reduce_scatter | solution.py:86
  110.0 188.6 %reduce-scatter.9.cloned.1.call-start = ((), (), s32[]{:S(2)}) async-start(), calls=%async_computation.6 | async-start | bytes 5242880 | tf_op jit(solution)/shard_map/reduce_scatter | solution.py:86
  160.8 217.3 %reduce-scatter.5.cloned.1.call-start = ((), (), s32[]{:S(2)}) async-start(), calls=%async_computation.4 | async-start | bytes 5242880 | tf_op jit(solution)/shard_map/reduce_scatter | solution.py:86
  163.0 7.7 %collective-permute-start = (bf16[3,2048,256]{2,1,0:T(8,128)(2,1)S(1)}, bf16[3,2048,256]{2,1,0:T(8,128)(2,1)S(1)}, u32[]{:S(2)}, u32[]{:S(2)}) collective-permute-start(bf16[3,2048,256]{2,1,0:T(8,128)(2,1)S(1)} %slice.22), channel_id=1, source_target_pairs={{0,4},{4,8},{8,12},{12,16},{16,20},{20,24},{24,28},{1,5},{5,9},{9,... | collective-permute-start | bytes 9437192 | tf_op jit(solution)/shard_map/ppermute | solution.py:18
  170.7 1.7 copy-start
  226.1 152.0 %copy-start.3 = (f32[2048]{0:T(1024)S(1)}, f32[2048]{0:T(1024)}, u32[]{:S(2)}) copy-start(f32[2048]{0:T(1024)} %param.13) | copy-start | bytes 24580
Sparse Core Ops, SparseCore 0:
  59.8 79.4 reduce-scatter.10
  141.7 77.2 reduce-scatter.6
  221.3 77.2 reduce-scatter.8
  300.9 77.2 reduce-scatter.4

commit v2 on v1

v2 whole, which is shorter than its diff:
```python
import functools

import jax
import jax.numpy as jnp
from jax import lax
from jax.experimental import pallas as pl
from jax.experimental.pallas import tpu as pltpu
from jax.sharding import PartitionSpec as P

STAPS = 7
MTAPS = 128
LANES = 128
F32 = jnp.float32
BF16 = jnp.bfloat16


def from_behind(value, axis, steps):
    count = lax.axis_size(axis)
    return lax.ppermute(value, axis, [(source, source + steps) for source in range(count - steps)])


def chunks(slab):
    plan = [(slab - LANES, LANES, False), (slab - 2 * LANES, LANES, False)]
    for first in range(slab - 4 * LANES, -1, -2 * LANES):
        plan.append((first, 2 * LANES, False))
    return plan


def feature_kernel(blocks, *refs):
    token_refs = refs[:blocks]
    short_ref, medium_ref, y_ref, wide, kv = refs[blocks:]
    for at, ref in enumerate(token_refs):
        for s in range(3):
            if s > 0 or at > 0:
                wide[s, at * LANES : (at + 1) * LANES] = ref[s].astype(F32).T

    def short(s, row):
        total = short_ref[s, 0:1] * wide[s, row : row + LANES]
        for j in range(1, STAPS):
            total = total + short_ref[s, j : j + 1] * wide[s, row - j : row - j + LANES]
        return total

    for at in range(1, blocks):
        row = at * LANES
        kv[row - LANES : row] = (short(1, row) * short(2, row)).astype(BF16).astype(F32)

    for at in range(blocks - 2):
        row = at * LANES
        total = jnp.zeros((LANES, LANES), F32)
        for low in range(8):
            start = row + 8 - low
            block = kv[start : start + LANES + MTAPS - 8]
            for high in range(0, MTAPS, 8):
                first = MTAPS - 8 - high
                total = total + medium_ref[high + low : high + low + 1] * block[first : first + LANES]
        y_ref[row : row + LANES] = (short(0, row + 2 * LANES) * total).astype(BF16)


def features(sources, short, medium):
    channels = short.shape[2]
    blocks = len(sources)
    tokens = (blocks - 2) * LANES
    return pl.pallas_call(
        functools.partial(feature_kernel, blocks),
        grid=(channels // LANES,),
        in_specs=[pl.BlockSpec((3, LANES, LANES), lambda c, at=at: (0, c, at)) for _, at in sources]
        + [
            pl.BlockSpec((3, STAPS, LANES), lambda c: (0, 0, c)),
            pl.BlockSpec((MTAPS, LANES), lambda c: (0, c)),
        ],
        out_specs=pl.BlockSpec((tokens, LANES), lambda c: (0, c)),
        out_shape=jax.ShapeDtypeStruct((tokens, channels), BF16),
        scratch_shapes=[
            pltpu.VMEM((3, blocks * LANES, LANES), F32),
            pltpu.VMEM(((blocks - 1) * LANES, LANES), F32),
        ],
        cost_estimate=pl.CostEstimate(
            flops=2 * channels * tokens * (MTAPS + 4 * STAPS),
            bytes_accessed=6 * channels * blocks * LANES,
            transcendentals=0,
        ),
    )(*[array for array, _ in sources], short, medium)


def finish_kernel(*refs):
    resid_ref, steer_ref, proj_ref, out_ref = refs[0], refs[1], refs[2], refs[-1]
    gain = proj_ref[...].astype(F32) + steer_ref[...]
    out_ref[...] = (resid_ref[...].astype(F32) + gain.T).astype(BF16)


def finish(resid, steer, proj, out, first):
    tokens, channels = proj.shape
    rows = min(channels, 512)
    at = first // tokens
    column = pl.BlockSpec((rows, tokens), lambda c: (c, at))
    specs = [
        column,
        pl.BlockSpec((1, rows), lambda c: (0, c)),
        pl.BlockSpec((tokens, rows), lambda c: (0, c)),
    ]
    held = [] if out is None else [out]
    return pl.pallas_call(
        finish_kernel,
        grid=(channels // rows,),
        in_specs=specs + [pl.BlockSpec(memory_space=pl.ANY)] * len(held),
        out_specs=column,
        out_shape=jax.ShapeDtypeStruct(resid.shape, BF16),
        input_output_aliases={3: 0} if held else {},
        cost_estimate=pl.CostEstimate(
            flops=2 * channels * tokens, bytes_accessed=6 * channels * tokens, transcendentals=0
        ),
    )(resid, steer, proj, *held)


def relay(part, axis):
    count = lax.axis_size(axis)
    me = lax.axis_index(axis)
    width = part.shape[1] // count

    def block(owner):
        return lax.dynamic_slice_in_dim(part, jnp.clip(owner, 0, count - 1) * width, width, 1)

    own = block(me).astype(F32)
    for way in (1, -1):
        total = None
        for step in range(count - 1):
            term = block(me + way * (count - 1 - step))
            if total is not None:
                term = (term.astype(F32) + total.astype(F32)).astype(BF16)
            pairs = [(z, z + 1) for z in range(step + 1)]
            if way < 0:
                pairs = [(count - 1 - a, count - 1 - b) for a, b in pairs]
            total = lax.ppermute(term, axis, pairs)
        own = own + total.astype(F32)
    return own.astype(BF16)


def shards(qkv, short_taps, medium_taps, skip_gain, w_out, resid, steer):
    slab = qkv.shape[2]
    short = jnp.swapaxes(short_taps.astype(F32), 1, 2)
    medium = medium_taps.astype(F32)
    medium = jnp.concatenate([medium[:, :1] + skip_gain[:, None], medium[:, 1:]], 1).T
    rim = from_behind(qkv[:, :, slab - 2 * LANES :], "seq", 1)
    out = None
    projs = []
    for first, tokens, by_relay in chunks(slab):
        at = first // LANES
        sources = [(rim, i + 2) if i < 0 else (qkv, i) for i in range(at - 2, at + tokens // LANES)]
        y = features(sources, short, medium)
        part = jnp.dot(y, w_out, preferred_element_type=F32).astype(BF16)
        if by_relay:
            proj = relay(part, "mp")
        else:
            proj = lax.psum_scatter(part, "mp", scatter_dimension=1, tiled=True)
        projs.append((first, proj))
    for first, proj in projs:
        out = finish(resid, steer[None], proj, out, first)
    return out


def solution(mesh):
    return jax.shard_map(
        shards,
        mesh=mesh,
        in_specs=(
            P(None, "mp", "seq"),
            P(None, "mp", None),
            P("mp", None),
            P("mp"),
            P("mp", None),
            P("mp", "seq"),
            P("mp"),
        ),
        out_specs=P("mp", "seq"),
        check_vma=False,
    )
```

time: 398 us -> 388 us (0.975)
  waiting for transfers between devices: 152 us -> 116 us
  Pallas kernels: 132 us -> 161 us
  matrix products: 68.3 us -> 83.9 us
  local copies, waits for them, and re-layouts: 20.7 us -> 5.2 us
  other arithmetic: 8.54 us -> 3.55 us
    reduce_scatter x4 -> x5, waiting for transfers between devices: 147 us -> 111 us  [shards(): proj = lax.psum_scatter(part, 'mp', scatter_dimension=1, tiled=True)]
    pallas_call x4 -> x10, Pallas kernels: 132 us -> 161 us  [the longest x5 142 us: features(): pl.pallas_call(functools.partial(feature_kernel, blocks), grid=(channels...]
    dot_general x4 -> x5, matrix products: 68.3 us -> 83.9 us  [shards(): part = jnp.dot(y, w_out, preferred_element_type=F32).astype(BF16)]
    concatenate x1 -> x0, local copies, waits for them, and re-layouts: 6.39 us -> none  [shards(): return jnp.concatenate(pieces, 1)]
    unnamed x13 -> x3, local copies, waits for them, and re-layouts: 8.21 us -> 2.91 us
    convert_element_type x1 -> x0, other arithmetic: 4.43 us -> none  [shards(): pieces[i] = (own + proj + steer[:, None]).astype(BF16)]
  transfers between devices with their start and end apart: 5 -> 6, of which waited for: 3 -> 3; matrix products, arithmetic and copies ran while one was open for 16% -> 18% of each run, Pallas kernels for 25% -> 36%
where the time goes in v2:
time: 388 us; the launch traced here: 387 us
  Pallas kernels  161 us (41%)
  waiting for transfers between devices  116 us (30%)
  matrix products  83.9 us (22%)
  between operations  13.2 us (3%)
  local copies, waits for them, and re-layouts  5.2 us (1%)
    pallas_call x5, Pallas kernels, features(): pl.pallas_call(functools.partial(feature_kernel, blocks), grid=(channels...  142 us
    reduce_scatter x5, waiting for transfers between devices, shards(): proj = lax.psum_scatter(part, 'mp', scatter_dimension=1, tiled=True)  111 us
    dot_general x5, matrix products, shards(): part = jnp.dot(y, w_out, preferred_element_type=F32).astype(BF16)  83.9 us
    pallas_call x5, Pallas kernels, finish(): pl.pallas_call(finish_kernel, grid=(channels // rows,), in_specs=specs +...  19.1 us
  transfers between devices with their start and end apart: 6, of which 3 were waited for; matrix products, arithmetic and copies ran while one was open for 18% of the time, Pallas kernels for 36%

profile of v2, /device:TPU:0, one launch (start us, length us, event | category | flops | bytes accessed | tf_op | source)
XLA Modules:
  0.0 386.7 jit_solution(4302340888421776244)
XLA Ops:
  6.5 0.0 reduce-scatter.14.cloned.1.call-start
  6.5 1.2 copy.12
  7.8 0.1 convert_element_type.19
  7.9 0.1 slice.13
  8.0 1.6 convert_bitcast_fusion.refs_4_.refs_3_
  9.6 0.7 slice_add_fusion
  10.3 1.2 maximum_bitcast_fusion.refs_5_.refs_4_
  11.5 18.4 %shard_map.77 = bf16[128,2048]{1,0:T(8,128)(2,1)} custom-call(bf16[3,2048,1024]{2,1,0:T(8,128)(2,1)} %refs_2_.9, bf16[3,2048,1024]{2,1,0:T(8,128)(2,1)} %refs_2_.9, bf16[3,2048,1024]{2,1,0:T(8,128)(2,1)} %refs_2_.9, f32[3,7,2048]{2,1,0:T(8,128)} %convert_bitcast_fusion.refs_4_.refs_3_, f32[128,2048]{1,0:T(8,128)} %maximum_bitcast_fusion.refs_5_.refs_4_), custom_call_target="tpu_custom_call" | custom-call | flops 81788928 | bytes 4718592 | tf_op jit(solution)/shard_map/pallas_call | solution.py:63
  29.9 16.6 %convolution_convert_fusion.3 = bf16[128,8192]{1,0:T(8,128)(2,1)} fusion(bf16[128,2048]{1,0:T(8,128)(2,1)} %shard_map.77, bf16[2048,8192]{1,0:T(8,128)(2,1)} %param.11), kind=kOutput, calls=%fused_computation.3 | convolution fusion | flops 4296015872 | bytes 36175872 | tf_op jit(solution)/shard_map/dot_general | solution.py:150
  46.5 0.0 reduce-scatter.14.cloned.1.call-update
  46.5 0.2 reduce-scatter.12.cloned.1.call-start
  46.7 18.4 %shard_map.76 = bf16[128,2048]{1,0:T(8,128)(2,1)} custom-call(bf16[3,2048,1024]{2,1,0:T(8,128)(2,1)} %refs_2_.9, bf16[3,2048,1024]{2,1,0:T(8,128)(2,1)} %refs_2_.9, bf16[3,2048,1024]{2,1,0:T(8,128)(2,1)} %refs_2_.9, f32[3,7,2048]{2,1,0:T(8,128)} %convert_bitcast_fusion.refs_4_.refs_3_, f32[128,2048]{1,0:T(8,128)} %maximum_bitcast_fusion.refs_5_.refs_4_), custom_call_target="tpu_custom_call" | custom-call | flops 81788928 | bytes 4718592 | tf_op jit(solution)/shard_map/pallas_call | solution.py:63
  65.2 16.7 %convolution_convert_fusion.4 = bf16[128,8192]{1,0:T(8,128)(2,1)} fusion(bf16[128,2048]{1,0:T(8,128)(2,1)} %shard_map.76, bf16[2048,8192]{1,0:T(8,128)(2,1)} %param.11), kind=kOutput, calls=%fused_computation.4 | convolution fusion | flops 4296015872 | bytes 36175872 | tf_op jit(solution)/shard_map/dot_general | solution.py:150
  81.9 0.0 reduce-scatter.12.cloned.1.call-update
  81.9 0.0 reduce-scatter.10.cloned.1.call-start
  82.0 35.1 %shard_map.75 = bf16[256,2048]{1,0:T(8,128)(2,1)} custom-call(bf16[3,2048,1024]{2,1,0:T(8,128)(2,1)} %refs_2_.9, bf16[3,2048,1024]{2,1,0:T(8,128)(2,1)} %refs_2_.9, bf16[3,2048,1024]{2,1,0:T(8,128)(2,1)} %refs_2_.9, bf16[3,2048,1024]{2,1,0:T(8,128)(2,1)} %refs_2_.9, f32[3,7,2048]{2,1,0:T(8,128)} %convert_bitcast_fusion.refs_4_.refs_3_, ...), custom_call_target="tpu_custom_call" | custom-call | flops 163577856 | bytes 6291456 | tf_op jit(solution)/shard_map/pallas_call | solution.py:63
  117.1 16.8 %convolution_convert_fusion = bf16[256,8192]{1,0:T(8,128)(2,1)} fusion(bf16[256,2048]{1,0:T(8,128)(2,1)} %shard_map.75, bf16[2048,8192]{1,0:T(8,128)(2,1)} %param.11), kind=kOutput, calls=%fused_computation | convolution fusion | flops 8592031744 | bytes 38797312 | tf_op jit(solution)/shard_map/dot_general | solution.py:150
  134.0 0.0 reduce-scatter.10.cloned.1.call-update
  134.0 0.3 reduce-scatter.8.cloned.1.call-start
  134.2 35.1 %shard_map.74 = bf16[256,2048]{1,0:T(8,128)(2,1)} custom-call(bf16[3,2048,1024]{2,1,0:T(8,128)(2,1)} %refs_2_.9, bf16[3,2048,1024]{2,1,0:T(8,128)(2,1)} %refs_2_.9, bf16[3,2048,1024]{2,1,0:T(8,128)(2,1)} %refs_2_.9, bf16[3,2048,1024]{2,1,0:T(8,128)(2,1)} %refs_2_.9, f32[3,7,2048]{2,1,0:T(8,128)} %convert_bitcast_fusion.refs_4_.refs_3_, ...), custom_call_target="tpu_custom_call" | custom-call | flops 163577856 | bytes 6291456 | tf_op jit(solution)/shard_map/pallas_call | solution.py:63
  169.4 16.8 %convolution_convert_fusion.1 = bf16[256,8192]{1,0:T(8,128)(2,1)} fusion(bf16[256,2048]{1,0:T(8,128)(2,1)} %shard_map.74, bf16[2048,8192]{1,0:T(8,128)(2,1)} %param.11), kind=kOutput, calls=%fused_computation.1 | convolution fusion | flops 8592031744 | bytes 38797312 | tf_op jit(solution)/shard_map/dot_general | solution.py:150
  186.2 0.0 reduce-scatter.8.cloned.1.call-update
  186.2 0.0 reduce-scatter.6.cloned.1.call-start
  186.2 2.2 slice.9
  188.4 2.8 collective-permute-start
  191.2 4.8 %collective-permute-done.refs_0_.refs_1_ = bf16[3,2048,256]{2,1,0:T(8,128)(2,1)S(1)} collective-permute-done((bf16[3,2048,256]{2,1,0:T(8,128)(2,1)S(1)}, bf16[3,2048,256]{2,1,0:T(8,128)(2,1)S(1)}, u32[]{:S(2)}, u32[]{:S(2)}) %collective-permute-start) | collective-permute-done | bytes 3145760 | tf_op jit(solution)/shard_map/ppermute | solution.py:19
  196.0 0.0 copy-start
  196.0 1.7 copy-done
  197.7 35.1 %shard_map.73 = bf16[256,2048]{1,0:T(8,128)(2,1)} custom-call(bf16[3,2048,256]{2,1,0:T(8,128)(2,1)} %copy-done, bf16[3,2048,256]{2,1,0:T(8,128)(2,1)} %copy-done, bf16[3,2048,1024]{2,1,0:T(8,128)(2,1)} %refs_2_.9, bf16[3,2048,1024]{2,1,0:T(8,128)(2,1)} %refs_2_.9, f32[3,7,2048]{2,1,0:T(8,128)} %convert_bitcast_fusion.refs_4_.refs_3_, ...), custom_call_target="tpu_custom_call" | custom-call | flops 163577856 | bytes 6291456 | tf_op jit(solution)/shard_map/pallas_call | solution.py:63
  232.8 16.9 %convolution_convert_fusion.2 = bf16[256,8192]{1,0:T(8,128)(2,1)} fusion(bf16[256,2048]{1,0:T(8,128)(2,1)} %shard_map.73, bf16[2048,8192]{1,0:T(8,128)(2,1)} %param.11), kind=kOutput, calls=%fused_computation.2 | convolution fusion | flops 8592031744 | bytes 38797312 | tf_op jit(solution)/shard_map/dot_general | solution.py:150
  249.8 0.0 reduce-scatter.6.cloned.1.call-update
  249.8 0.0 reduce-scatter.14.cloned.1.call-done.refs_2_
  249.8 3.6 shard_map.78.refs_3_
  253.4 0.0 reduce-scatter.12.cloned.1.call-done.refs_2_
  253.4 3.6 shard_map.79.refs_3_
  257.0 0.0 reduce-scatter.10.cloned.1.call-done.refs_2_
  257.0 4.0 %shard_map.80.refs_3_ = bf16[2048,1024]{1,0:T(8,128)(2,1)} custom-call(bf16[2048,1024]{1,0:T(8,128)(2,1)} %refs_0_.17, f32[1,2048]{1,0:T(1,128)} %bitcast.18, bf16[256,2048]{1,0:T(8,128)(2,1)} %reduce-scatter.10.cloned.1.call-done.refs_2_, bf16[2048,1024]{1,0:T(8,128)(2,1)} %shard_map.79.refs_3_), custom_call_target="tpu_custom_call", output_to_operand_aliasing={{}: (3, {})} | custom-call | flops 1048576 | bytes 3145728 | tf_op jit(solution)/shard_map/pallas_call | solution.py:102
  261.0 35.8 %reduce-scatter.8.cloned.1.call-done.refs_2_ = bf16[256,2048]{1,0:T(8,128)(2,1)} async-done(((bf16[256,8192]{1,0:T(8,128)(2,1)}), bf16[256,2048]{1,0:T(8,128)(2,1)}) %reduce-scatter.8.cloned.1.call-update) | async-done | bytes 1048592 | tf_op jit(solution)/shard_map/reduce_scatter | solution.py:154
  296.8 4.0 %shard_map.81.refs_3_ = bf16[2048,1024]{1,0:T(8,128)(2,1)} custom-call(bf16[2048,1024]{1,0:T(8,128)(2,1)} %refs_0_.17, f32[1,2048]{1,0:T(1,128)} %bitcast.19, bf16[256,2048]{1,0:T(8,128)(2,1)} %reduce-scatter.8.cloned.1.call-done.refs_2_, bf16[2048,1024]{1,0:T(8,128)(2,1)} %shard_map.80.refs_3_), custom_call_target="tpu_custom_call", output_to_operand_aliasing={{}: (3, {})} | custom-call | flops 1048576 | bytes 3145728 | tf_op jit(solution)/shard_map/pallas_call | solution.py:102
  300.7 75.5 %reduce-scatter.6.cloned.1.call-done.refs_2_ = bf16[256,2048]{1,0:T(8,128)(2,1)} async-done(((bf16[256,8192]{1,0:T(8,128)(2,1)}), bf16[256,2048]{1,0:T(8,128)(2,1)}) %reduce-scatter.6.cloned.1.call-update) | async-done | bytes 1048592 | tf_op jit(solution)/shard_map/reduce_scatter | solution.py:154
  376.2 4.0 %shard_map.82 = bf16[2048,1024]{1,0:T(8,128)(2,1)} custom-call(bf16[2048,1024]{1,0:T(8,128)(2,1)} %refs_0_.17, f32[1,2048]{1,0:T(1,128)} %bitcast.20, bf16[256,2048]{1,0:T(8,128)(2,1)} %reduce-scatter.6.cloned.1.call-done.refs_2_, bf16[2048,1024]{1,0:T(8,128)(2,1)} %shard_map.81.refs_3_), custom_call_target="tpu_custom_call", output_to_operand_aliasing={{}: (3, {})} | custom-call | flops 1048576 | bytes 3145728 | tf_op jit(solution)/shard_map/pallas_call | solution.py:102
Async XLA Ops:
  6.5 243.3 %reduce-scatter.14.cloned.1.call-start = ((), (), s32[]{:S(2)}) async-start(), calls=%async_computation.9 | async-start | bytes 2621440 | tf_op jit(solution)/shard_map/reduce_scatter | solution.py:154
  46.5 206.9 %reduce-scatter.12.cloned.1.call-start = ((), (), s32[]{:S(2)}) async-start(), calls=%async_computation.8 | async-start | bytes 2621440 | tf_op jit(solution)/shard_map/reduce_scatter | solution.py:154
  81.9 175.1 %reduce-scatter.10.cloned.1.call-start = ((), (), s32[]{:S(2)}) async-start(), calls=%async_computation.7 | async-start | bytes 5242880 | tf_op jit(solution)/shard_map/reduce_scatter | solution.py:154
  134.0 162.8 %reduce-scatter.8.cloned.1.call-start = ((), (), s32[]{:S(2)}) async-start(), calls=%async_computation.6 | async-start | bytes 5242880 | tf_op jit(solution)/shard_map/reduce_scatter | solution.py:154
  186.2 190.0 %reduce-scatter.6.cloned.1.call-start = ((), (), s32[]{:S(2)}) async-start(), calls=%async_computation.5 | async-start | bytes 5242880 | tf_op jit(solution)/shard_map/reduce_scatter | solution.py:154
  188.4 7.6 %collective-permute-start = (bf16[3,2048,256]{2,1,0:T(8,128)(2,1)S(1)}, bf16[3,2048,256]{2,1,0:T(8,128)(2,1)S(1)}, u32[]{:S(2)}, u32[]{:S(2)}) collective-permute-start(bf16[3,2048,256]{2,1,0:T(8,128)(2,1)S(1)} %slice.9), channel_id=1, source_target_pairs={{0,4},{4,8},{8,12},{12,16},{16,20},{20,24},{24,28},{1,5},{5,9},{9,... | collective-permute-start | bytes 9437192 | tf_op jit(solution)/shard_map/ppermute | solution.py:19
  196.0 1.7 copy-start
Sparse Core Ops, SparseCore 0:
  46.6 46.5 reduce-scatter.13
  95.6 43.1 reduce-scatter.11
  141.1 76.0 reduce-scatter.9
  219.5 77.2 reduce-scatter.7
  298.9 77.2 reduce-scatter.5

commit v3 on v2

--- a/solution.py
+++ b/solution.py
@@ -20,10 +20,10 @@
 
 
 def chunks(slab):
-    plan = [(slab - LANES, LANES, False), (slab - 2 * LANES, LANES, False)]
-    for first in range(slab - 4 * LANES, -1, -2 * LANES):
-        plan.append((first, 2 * LANES, False))
-    return plan
+    plan = [(slab - LANES, LANES, False)]
+    for first in range(slab - 3 * LANES, 0, -2 * LANES):
+        plan.append((first, 2 * LANES, first == LANES))
+    return plan + [(0, LANES, False)]
 
 
 def feature_kernel(blocks, *refs):
@@ -90,18 +90,18 @@
 
 def finish(resid, steer, proj, out, first):
     tokens, channels = proj.shape
-    rows = min(channels, 512)
-    at = first // tokens
-    column = pl.BlockSpec((rows, tokens), lambda c: (c, at))
+    rows = min(channels, 1024)
+    at = first // LANES
+    column = pl.BlockSpec((rows, LANES), lambda t, c: (c, at + t))
     specs = [
         column,
-        pl.BlockSpec((1, rows), lambda c: (0, c)),
-        pl.BlockSpec((tokens, rows), lambda c: (0, c)),
+        pl.BlockSpec((1, rows), lambda t, c: (0, c)),
+        pl.BlockSpec((LANES, rows), lambda t, c: (t, c)),
     ]
     held = [] if out is None else [out]
     return pl.pallas_call(
         finish_kernel,
-        grid=(channels // rows,),
+        grid=(tokens // LANES, channels // rows),
         in_specs=specs + [pl.BlockSpec(memory_space=pl.ANY)] * len(held),
         out_specs=column,
         out_shape=jax.ShapeDtypeStruct(resid.shape, BF16),

time: 388 us -> 409 us (1.054)
  starting transfers between devices: 3.39 us -> 20.8 us
  other arithmetic: 3.55 us -> 11.9 us
  waiting for transfers between devices: 116 us -> 111 us
    reduce_scatter x5 -> x4, waiting for transfers between devices: 111 us -> 0.03 us  [shards(): proj = lax.psum_scatter(part, 'mp', scatter_dimension=1, tiled=True)]
    ppermute x0 -> x6, waiting for transfers between devices: none -> 111 us  [relay(): total = lax.ppermute(term, axis, pairs)]
    ppermute x0 -> x6, starting transfers between devices: none -> 17.7 us  [relay(): total = lax.ppermute(term, axis, pairs)]
    convert_element_type x0 -> x4, other arithmetic: none -> 10 us  [the longest x3 7.22 us: relay(): term = (term.astype(F32) + total.astype(F32)).astype(BF16)]
    ppermute x1, waiting for transfers between devices: 4.81 us -> 0.01 us  [from_behind(): lax.ppermute(value, axis, [(source, source + steps) for source in range(c...]
  transfers between devices with their start and end apart: 6 -> 11, of which waited for: 3 -> 4; matrix products, arithmetic and copies ran while one was open for 18% -> 20% of each run, Pallas kernels for 36% -> 34%
where the time goes in v3:
time: 409 us; the launch traced here: 407 us
  Pallas kernels  159 us (39%)
  waiting for transfers between devices  111 us (27%)
  matrix products  82.4 us (20%)
  starting transfers between devices  20.8 us (5%)
  between operations  13.3 us (3%)
  other arithmetic  11.9 us (3%)
  local copies, waits for them, and re-layouts  8.94 us (2%)
    pallas_call x5, Pallas kernels, features(): pl.pallas_call(functools.partial(feature_kernel, blocks), grid=(channels...  142 us
    ppermute x6, waiting for transfers between devices, relay(): total = lax.ppermute(term, axis, pairs)  111 us
    dot_general x5, matrix products, shards(): part = jnp.dot(y, w_out, preferred_element_type=F32).astype(BF16)  82.4 us
    ppermute x6, starting transfers between devices, relay(): total = lax.ppermute(term, axis, pairs)  17.7 us
    pallas_call x5, Pallas kernels, finish(): pl.pallas_call(finish_kernel, grid=(tokens // LANES, channels // rows), i...  16.3 us
  transfers between devices with their start and end apart: 11, of which 4 were waited for; matrix products, arithmetic and copies ran while one was open for 20% of the time, Pallas kernels for 34%

profile of v3, /device:TPU:0, one launch (start us, length us, event | category | flops | bytes accessed | tf_op | source)
XLA Modules:
  0.0 407.1 jit_solution(9322641889618334298)
XLA Ops:
  6.5 0.0 copy-start.2
  6.5 0.0 copy-start.3
  6.5 0.0 reduce-scatter.11.cloned.1.call-start
  6.5 1.3 copy.12
  7.8 0.1 slice.13
  8.0 0.1 convert_element_type.67
  8.1 0.0 copy-done.2
  8.1 0.7 convert_bitcast_fusion.refs_3_.refs_4_
  8.8 0.0 copy-done.3
  8.8 1.1 maximum_bitcast_fusion.refs_4_.refs_5_
  9.9 18.4 %shard_map.77 = bf16[128,2048]{1,0:T(8,128)(2,1)} custom-call(bf16[3,2048,1024]{2,1,0:T(8,128)(2,1)} %refs_2_.9, bf16[3,2048,1024]{2,1,0:T(8,128)(2,1)} %refs_2_.9, bf16[3,2048,1024]{2,1,0:T(8,128)(2,1)} %refs_2_.9, f32[3,7,2048]{2,1,0:T(8,128)} %convert_bitcast_fusion.refs_3_.refs_4_, f32[128,2048]{1,0:T(8,128)} %maximum_bitcast_fusion.refs_4_.refs_5_), custom_call_target="tpu_custom_call" | custom-call | flops 81788928 | bytes 4718592 | tf_op jit(solution)/shard_map/pallas_call | solution.py:63
  28.3 16.6 %convolution_convert_fusion.3 = bf16[128,8192]{1,0:T(8,128)(2,1)} fusion(bf16[128,2048]{1,0:T(8,128)(2,1)} %shard_map.77, bf16[2048,8192]{1,0:T(8,128)(2,1)} %param.11), kind=kOutput, calls=%fused_computation.3 | convolution fusion | flops 4296015872 | bytes 36175872 | tf_op jit(solution)/shard_map/dot_general | solution.py:150
  44.9 0.0 reduce-scatter.11.cloned.1.call-update
  44.9 0.2 reduce-scatter.9.cloned.1.call-start
  45.1 35.1 %shard_map.76 = bf16[256,2048]{1,0:T(8,128)(2,1)} custom-call(bf16[3,2048,1024]{2,1,0:T(8,128)(2,1)} %refs_2_.9, bf16[3,2048,1024]{2,1,0:T(8,128)(2,1)} %refs_2_.9, bf16[3,2048,1024]{2,1,0:T(8,128)(2,1)} %refs_2_.9, bf16[3,2048,1024]{2,1,0:T(8,128)(2,1)} %refs_2_.9, f32[3,7,2048]{2,1,0:T(8,128)} %convert_bitcast_fusion.refs_3_.refs_4_, ...), custom_call_target="tpu_custom_call" | custom-call | flops 163577856 | bytes 6291456 | tf_op jit(solution)/shard_map/pallas_call | solution.py:63
  80.3 16.8 %convolution_convert_fusion = bf16[256,8192]{1,0:T(8,128)(2,1)} fusion(bf16[256,2048]{1,0:T(8,128)(2,1)} %shard_map.76, bf16[2048,8192]{1,0:T(8,128)(2,1)} %param.11), kind=kOutput, calls=%fused_computation | convolution fusion | flops 8592031744 | bytes 38797312 | tf_op jit(solution)/shard_map/dot_general | solution.py:150
  97.1 0.0 reduce-scatter.9.cloned.1.call-update
  97.1 0.0 reduce-scatter.7.cloned.1.call-start
  97.1 3.8 slice.9
  100.9 2.6 collective-permute-start
  103.5 35.2 %shard_map.75 = bf16[256,2048]{1,0:T(8,128)(2,1)} custom-call(bf16[3,2048,1024]{2,1,0:T(8,128)(2,1)} %refs_2_.9, bf16[3,2048,1024]{2,1,0:T(8,128)(2,1)} %refs_2_.9, bf16[3,2048,1024]{2,1,0:T(8,128)(2,1)} %refs_2_.9, bf16[3,2048,1024]{2,1,0:T(8,128)(2,1)} %refs_2_.9, f32[3,7,2048]{2,1,0:T(8,128)} %convert_bitcast_fusion.refs_3_.refs_4_, ...), custom_call_target="tpu_custom_call" | custom-call | flops 163577856 | bytes 6291456 | tf_op jit(solution)/shard_map/pallas_call | solution.py:63
  138.6 16.9 %convolution_convert_fusion.1 = bf16[256,8192]{1,0:T(8,128)(2,1)} fusion(bf16[256,2048]{1,0:T(8,128)(2,1)} %shard_map.75, bf16[2048,8192]{1,0:T(8,128)(2,1)} %param.11), kind=kOutput, calls=%fused_computation.1 | convolution fusion | flops 8592031744 | bytes 38797312 | tf_op jit(solution)/shard_map/dot_general | solution.py:150
  155.5 0.0 reduce-scatter.7.cloned.1.call-update
  155.5 0.3 reduce-scatter.5.cloned.1.call-start
  155.8 0.0 collective-permute-done.refs_0_.refs_1_
  155.8 0.0 copy-start
  155.8 1.7 copy-done
  157.5 35.1 %shard_map.74 = bf16[256,2048]{1,0:T(8,128)(2,1)} custom-call(bf16[3,2048,256]{2,1,0:T(8,128)(2,1)} %copy-done, bf16[3,2048,1024]{2,1,0:T(8,128)(2,1)} %refs_2_.9, bf16[3,2048,1024]{2,1,0:T(8,128)(2,1)} %refs_2_.9, bf16[3,2048,1024]{2,1,0:T(8,128)(2,1)} %refs_2_.9, f32[3,7,2048]{2,1,0:T(8,128)} %convert_bitcast_fusion.refs_3_.refs_4_, ...), custom_call_target="tpu_custom_call" | custom-call | flops 163577856 | bytes 6291456 | tf_op jit(solution)/shard_map/pallas_call | solution.py:63
  192.6 15.5 %convolution_convert_fusion.2 = bf16[256,8192]{1,0:T(8,128)(2,1)S(1)} fusion(bf16[256,2048]{1,0:T(8,128)(2,1)} %shard_map.74, bf16[2048,8192]{1,0:T(8,128)(2,1)} %param.11), kind=kOutput, calls=%fused_computation.2 | convolution fusion | flops 8592031744 | bytes 38797312 | tf_op jit(solution)/shard_map/dot_general | solution.py:150
  208.1 0.0 copy-start.1
  208.2 2.0 copy-done.1
  210.1 0.1 constant_dynamic-slice_fusion.1
  210.3 4.4 %collective-permute-start.1 = (bf16[256,2048]{1,0:T(8,128)(2,1)S(1)}, bf16[256,2048]{1,0:T(8,128)(2,1)S(1)}, u32[]{:S(2)}, u32[]{:S(2)}) collective-permute-start(bf16[256,2048]{1,0:T(8,128)(2,1)S(1)} %get-tuple-element.7), channel_id=1, source_target_pairs={{0,1},{4,5},{8,9},{12,13},{16,17},{20,21},{24,25},{28,29}} | collective-permute-start | bytes 3145736 | tf_op jit(solution)/shard_map/ppermute | solution.py:133
  214.6 1.6 collective-permute-start.4
  216.3 18.4 %shard_map.73 = bf16[128,2048]{1,0:T(8,128)(2,1)} custom-call(bf16[3,2048,256]{2,1,0:T(8,128)(2,1)} %copy-done, bf16[3,2048,256]{2,1,0:T(8,128)(2,1)} %copy-done, bf16[3,2048,1024]{2,1,0:T(8,128)(2,1)} %refs_2_.9, f32[3,7,2048]{2,1,0:T(8,128)} %convert_bitcast_fusion.refs_3_.refs_4_, f32[128,2048]{1,0:T(8,128)} %maximum_bitcast_fusion.refs_4_.refs_5_), custom_call_target="tpu_custom_call" | custom-call | flops 81788928 | bytes 4718592 | tf_op jit(solution)/shard_map/pallas_call | solution.py:63
  234.7 25.8 %collective-permute-done.1 = bf16[256,2048]{1,0:T(8,128)(2,1)S(1)} collective-permute-done((bf16[256,2048]{1,0:T(8,128)(2,1)S(1)}, bf16[256,2048]{1,0:T(8,128)(2,1)S(1)}, u32[]{:S(2)}, u32[]{:S(2)}) %collective-permute-start.1) | collective-permute-done | bytes 1048608 | tf_op jit(solution)/shard_map/ppermute | solution.py:133
  260.5 1.6 add_convert_fusion.4
  262.1 4.7 %collective-permute-start.2 = (bf16[256,2048]{1,0:T(8,128)(2,1)S(1)}, bf16[256,2048]{1,0:T(8,128)(2,1)S(1)}, u32[]{:S(2)}, u32[]{:S(2)}) collective-permute-start(bf16[256,2048]{1,0:T(8,128)(2,1)S(1)} %add_convert_fusion.4), channel_id=1, source_target_pairs={{0,1},{1,2},{4,5},{5,6},{8,9},{9,10},{12,13},{13,14},{16,17},{17,1... | collective-permute-start | bytes 3145736 | tf_op jit(solution)/shard_map/ppermute | solution.py:133
  266.8 16.6 %convolution_convert_fusion.4 = bf16[128,8192]{1,0:T(8,128)(2,1)} fusion(bf16[128,2048]{1,0:T(8,128)(2,1)} %shard_map.73, bf16[2048,8192]{1,0:T(8,128)(2,1)} %param.11), kind=kOutput, calls=%fused_computation.4 | convolution fusion | flops 4296015872 | bytes 36175872 | tf_op jit(solution)/shard_map/dot_general | solution.py:150
  283.5 0.0 reduce-scatter.5.cloned.1.call-update
  283.5 0.0 collective-permute-done.4
  283.5 15.1 %collective-permute-done.2 = bf16[256,2048]{1,0:T(8,128)(2,1)S(1)} collective-permute-done((bf16[256,2048]{1,0:T(8,128)(2,1)S(1)}, bf16[256,2048]{1,0:T(8,128)(2,1)S(1)}, u32[]{:S(2)}, u32[]{:S(2)}) %collective-permute-start.2) | collective-permute-done | bytes 1048608 | tf_op jit(solution)/shard_map/ppermute | solution.py:133
  298.6 4.0 add_convert_fusion.3
  302.6 0.7 collective-permute-start.5
  303.4 5.0 %collective-permute-start.3 = (bf16[256,2048]{1,0:T(8,128)(2,1)}, bf16[256,2048]{1,0:T(8,128)(2,1)S(1)}, u32[]{:S(2)}, u32[]{:S(2)}) collective-permute-start(bf16[256,2048]{1,0:T(8,128)(2,1)} %get-tuple-element.5), channel_id=1, source_target_pairs={{0,1},{1,2},{2,3},{4,5},{5,6},{6,7},{8,9},{9,10},{10,11},{12,13},{... | collective-permute-start | bytes 3145736 | tf_op jit(solution)/shard_map/ppermute | solution.py:133
  308.4 0.0 collective-permute-done.5
  308.4 1.6 add_convert_fusion.1
  310.0 1.3 collective-permute-start.6
  311.3 0.0 reduce-scatter.11.cloned.1.call-done.refs_2_
  311.3 2.2 shard_map.78.refs_3_
  313.6 40.8 %collective-permute-done.3 = bf16[256,2048]{1,0:T(8,128)(2,1)S(1)} collective-permute-done((bf16[256,2048]{1,0:T(8,128)(2,1)}, bf16[256,2048]{1,0:T(8,128)(2,1)S(1)}, u32[]{:S(2)}, u32[]{:S(2)}) %collective-permute-start.3) | collective-permute-done | bytes 1048608 | tf_op jit(solution)/shard_map/ppermute | solution.py:133
  354.4 29.3 %collective-permute-done.6 = bf16[256,2048]{1,0:T(8,128)(2,1)S(1)} collective-permute-done((bf16[256,2048]{1,0:T(8,128)(2,1)S(1)}, bf16[256,2048]{1,0:T(8,128)(2,1)S(1)}, u32[]{:S(2)}, u32[]{:S(2)}) %collective-permute-start.6) | collective-permute-done | bytes 1048608 | tf_op jit(solution)/shard_map/ppermute | solution.py:133
  383.7 2.8 add_convert_fusion.refs_2_
  386.5 0.0 reduce-scatter.9.cloned.1.call-done.refs_2_
  386.5 4.0 shard_map.79.refs_3_
  390.5 0.0 reduce-scatter.7.cloned.1.call-done.refs_2_
  390.5 4.0 shard_map.80.refs_3_
  394.5 4.0 shard_map.81.refs_3_
  398.4 0.0 reduce-scatter.5.cloned.1.call-done.refs_2_
  398.4 2.2 shard_map.82
  (1 shorter events, 0.0 us)
Async XLA Ops:
  6.5 1.5 copy-start.2
  6.5 2.2 copy-start.3
  6.5 304.8 %reduce-scatter.11.cloned.1.call-start = ((), (), s32[]{:S(2)}) async-start(), calls=%async_computation.7 | async-start | bytes 2621440 | tf_op jit(solution)/shard_map/reduce_scatter | solution.py:154
  44.9 341.6 %reduce-scatter.9.cloned.1.call-start = ((), (), s32[]{:S(2)}) async-start(), calls=%async_computation.6 | async-start | bytes 5242880 | tf_op jit(solution)/shard_map/reduce_scatter | solution.py:154
  97.1 293.4 %reduce-scatter.7.cloned.1.call-start = ((), (), s32[]{:S(2)}) async-start(), calls=%async_computation.5 | async-start | bytes 5242880 | tf_op jit(solution)/shard_map/reduce_scatter | solution.py:154
  100.9 54.9 %collective-permute-start = (bf16[3,2048,256]{2,1,0:T(8,128)(2,1)}, bf16[3,2048,256]{2,1,0:T(8,128)(2,1)S(1)}, u32[]{:S(2)}, u32[]{:S(2)}) collective-permute-start(bf16[3,2048,256]{2,1,0:T(8,128)(2,1)} %slice.9), channel_id=1, source_target_pairs={{0,4},{4,8},{8,12},{12,16},{16,20},{20,24},{24,28},{1,5},{5,9},{9,... | collective-permute-start | bytes 9437192 | tf_op jit(solution)/shard_map/ppermute | solution.py:19
  155.5 242.9 %reduce-scatter.5.cloned.1.call-start = ((), (), s32[]{:S(2)}) async-start(), calls=%async_computation.4 | async-start | bytes 2621440 | tf_op jit(solution)/shard_map/reduce_scatter | solution.py:154
  155.8 1.7 copy-start
  208.1 2.0 copy-start.1
  210.3 50.2 %collective-permute-start.1 = (bf16[256,2048]{1,0:T(8,128)(2,1)S(1)}, bf16[256,2048]{1,0:T(8,128)(2,1)S(1)}, u32[]{:S(2)}, u32[]{:S(2)}) collective-permute-start(bf16[256,2048]{1,0:T(8,128)(2,1)S(1)} %get-tuple-element.7), channel_id=1, source_target_pairs={{0,1},{4,5},{8,9},{12,13},{16,17},{20,21},{24,25},{28,29}} | collective-permute-start | bytes 3145736 | tf_op jit(solution)/shard_map/ppermute | solution.py:133
  214.6 68.9 %collective-permute-start.4 = (bf16[256,2048]{1,0:T(8,128)(2,1)S(1)}, bf16[256,2048]{1,0:T(8,128)(2,1)}, u32[]{:S(2)}, u32[]{:S(2)}) collective-permute-start(bf16[256,2048]{1,0:T(8,128)(2,1)S(1)} %get-tuple-element.8), channel_id=1, source_target_pairs={{3,2},{7,6},{11,10},{15,14},{19,18},{23,22},{27,26},{31,30}} | collective-permute-start | bytes 3145736 | tf_op jit(solution)/shard_map/ppermute | solution.py:133
  262.1 36.5 %collective-permute-start.2 = (bf16[256,2048]{1,0:T(8,128)(2,1)S(1)}, bf16[256,2048]{1,0:T(8,128)(2,1)S(1)}, u32[]{:S(2)}, u32[]{:S(2)}) collective-permute-start(bf16[256,2048]{1,0:T(8,128)(2,1)S(1)} %add_convert_fusion.4), channel_id=1, source_target_pairs={{0,1},{1,2},{4,5},{5,6},{8,9},{9,10},{12,13},{13,14},{16,17},{17,1... | collective-permute-start | bytes 3145736 | tf_op jit(solution)/shard_map/ppermute | solution.py:133
  302.6 5.8 %collective-permute-start.5 = (bf16[256,2048]{1,0:T(8,128)(2,1)}, bf16[256,2048]{1,0:T(8,128)(2,1)S(1)}, u32[]{:S(2)}, u32[]{:S(2)}) collective-permute-start(bf16[256,2048]{1,0:T(8,128)(2,1)} %get-tuple-element.6), channel_id=1, source_target_pairs={{3,2},{2,1},{7,6},{6,5},{11,10},{10,9},{15,14},{14,13},{19,18},{18... | collective-permute-start | bytes 3145736 | tf_op jit(solution)/shard_map/ppermute | solution.py:133
  303.4 51.0 %collective-permute-start.3 = (bf16[256,2048]{1,0:T(8,128)(2,1)}, bf16[256,2048]{1,0:T(8,128)(2,1)S(1)}, u32[]{:S(2)}, u32[]{:S(2)}) collective-permute-start(bf16[256,2048]{1,0:T(8,128)(2,1)} %get-tuple-element.5), channel_id=1, source_target_pairs={{0,1},{1,2},{2,3},{4,5},{5,6},{6,7},{8,9},{9,10},{10,11},{12,13},{... | collective-permute-start | bytes 3145736 | tf_op jit(solution)/shard_map/ppermute | solution.py:133
  310.0 73.7 %collective-permute-start.6 = (bf16[256,2048]{1,0:T(8,128)(2,1)S(1)}, bf16[256,2048]{1,0:T(8,128)(2,1)S(1)}, u32[]{:S(2)}, u32[]{:S(2)}) collective-permute-start(bf16[256,2048]{1,0:T(8,128)(2,1)S(1)} %add_convert_fusion.1), channel_id=1, source_target_pairs={{3,2},{2,1},{1,0},{7,6},{6,5},{5,4},{11,10},{10,9},{9,8},{15,14},{... | collective-permute-start | bytes 3145736 | tf_op jit(solution)/shard_map/ppermute | solution.py:133
Sparse Core Ops, SparseCore 0:
  45.0 46.5 reduce-scatter.10
  97.2 79.4 reduce-scatter.8
  179.0 105.7 reduce-scatter.6
  287.0 70.3 reduce-scatter.4

commit v4 on v3

--- a/solution.py
+++ b/solution.py
@@ -20,10 +20,17 @@
 
 
 def chunks(slab):
-    plan = [(slab - LANES, LANES, False)]
-    for first in range(slab - 3 * LANES, 0, -2 * LANES):
-        plan.append((first, 2 * LANES, first == LANES))
-    return plan + [(0, LANES, False)]
+    sizes = [1]
+    left = slab // LANES - 3
+    while left > 0:
+        sizes.append(min(left, 2 if len(sizes) == 1 else 3))
+        left -= sizes[-1]
+    sizes.append(2)
+    plan, end = [], slab
+    for size in sizes:
+        end -= size * LANES
+        plan.append((end, size * LANES))
+    return plan
 
 
 def feature_kernel(blocks, *refs):
@@ -112,29 +119,6 @@
     )(resid, steer, proj, *held)
 
 
-def relay(part, axis):
-    count = lax.axis_size(axis)
-    me = lax.axis_index(axis)
-    width = part.shape[1] // count
-
-    def block(owner):
-        return lax.dynamic_slice_in_dim(part, jnp.clip(owner, 0, count - 1) * width, width, 1)
-
-    own = block(me).astype(F32)
-    for way in (1, -1):
-        total = None
-        for step in range(count - 1):
-            term = block(me + way * (count - 1 - step))
-            if total is not None:
-                term = (term.astype(F32) + total.astype(F32)).astype(BF16)
-            pairs = [(z, z + 1) for z in range(step + 1)]
-            if way < 0:
-                pairs = [(count - 1 - a, count - 1 - b) for a, b in pairs]
-            total = lax.ppermute(term, axis, pairs)
-        own = own + total.astype(F32)
-    return own.astype(BF16)
-
-
 def shards(qkv, short_taps, medium_taps, skip_gain, w_out, resid, steer):
     slab = qkv.shape[2]
     short = jnp.swapaxes(short_taps.astype(F32), 1, 2)
@@ -143,15 +127,12 @@
     rim = from_behind(qkv[:, :, slab - 2 * LANES :], "seq", 1)
     out = None
     projs = []
-    for first, tokens, by_relay in chunks(slab):
+    for first, tokens in chunks(slab):
         at = first // LANES
         sources = [(rim, i + 2) if i < 0 else (qkv, i) for i in range(at - 2, at + tokens // LANES)]
         y = features(sources, short, medium)
         part = jnp.dot(y, w_out, preferred_element_type=F32).astype(BF16)
-        if by_relay:
-            proj = relay(part, "mp")
-        else:
-            proj = lax.psum_scatter(part, "mp", scatter_dimension=1, tiled=True)
+        proj = lax.psum_scatter(part, "mp", scatter_dimension=1, tiled=True)
         projs.append((first, proj))
     for first, proj in projs:
         out = finish(resid, steer[None], proj, out, first)

time: 409 us -> 383 us (0.936)
  waiting for transfers between devices: 111 us -> 134 us
  starting transfers between devices: 20.8 us -> 3.37 us
  matrix products: 82.4 us -> 71.5 us
  other arithmetic: 11.9 us -> 3.46 us
  Pallas kernels: 159 us -> 151 us
    reduce_scatter x4, waiting for transfers between devices: 0.03 us -> 129 us  [shards(): proj = lax.psum_scatter(part, 'mp', scatter_dimension=1, tiled=True)]
    ppermute x6 -> x0, waiting for transfers between devices: 111 us -> none  [relay(): total = lax.ppermute(term, axis, pairs)]
    ppermute x6 -> x0, starting transfers between devices: 17.7 us -> none  [relay(): total = lax.ppermute(term, axis, pairs)]
    dot_general x5 -> x4, matrix products: 82.4 us -> 71.5 us  [shards(): part = jnp.dot(y, w_out, preferred_element_type=F32).astype(BF16)]
    convert_element_type x4 -> x0, other arithmetic: 10 us -> none  [the longest x3 7.22 us: relay(): term = (term.astype(F32) + total.astype(F32)).astype(BF16)]
    pallas_call x5 -> x4, Pallas kernels: 142 us -> 136 us  [features(): pl.pallas_call(functools.partial(feature_kernel, blocks), grid=(channels...]
    ppermute x1, waiting for transfers between devices: 0.01 us -> 4.81 us  [from_behind(): lax.ppermute(value, axis, [(source, source + steps) for source in range(c...]
    pallas_call x5 -> x4, Pallas kernels: 16.3 us -> 15.6 us  [finish(): pl.pallas_call(finish_kernel, grid=(tokens // LANES, channels // rows), i...]
  transfers between devices with their start and end apart: 11 -> 5, of which waited for: 4 -> 3; matrix products, arithmetic and copies ran while one was open for 20% -> 15% of each run, Pallas kernels for 34% -> 34%
where the time goes in v4:
time: 383 us; the launch traced here: 382 us
  Pallas kernels  151 us (39%)
  waiting for transfers between devices  134 us (35%)
  matrix products  71.5 us (19%)
  between operations  13.2 us (3%)
  local copies, waits for them, and re-layouts  5.14 us (1%)
    pallas_call x4, Pallas kernels, features(): pl.pallas_call(functools.partial(feature_kernel, blocks), grid=(channels...  136 us
    reduce_scatter x4, waiting for transfers between devices, shards(): proj = lax.psum_scatter(part, 'mp', scatter_dimension=1, tiled=True)  129 us
    dot_general x4, matrix products, shards(): part = jnp.dot(y, w_out, preferred_element_type=F32).astype(BF16)  71.5 us
    pallas_call x4, Pallas kernels, finish(): pl.pallas_call(finish_kernel, grid=(tokens // LANES, channels // rows), i...  15.6 us
  transfers between devices with their start and end apart: 5, of which 3 were waited for; matrix products, arithmetic and copies ran while one was open for 15% of the time, Pallas kernels for 34%

profile of v4, /device:TPU:0, one launch (start us, length us, event | category | flops | bytes accessed | tf_op | source)
XLA Modules:
  0.0 381.8 jit_solution(6992846496144260121)
XLA Ops:
  6.5 0.0 reduce-scatter.11.cloned.1.call-start
  6.5 1.2 copy.11
  7.8 0.1 slice.13
  7.9 0.1 convert_element_type.16
  8.0 1.6 convert_bitcast_fusion.refs_4_.refs_5_.refs_3_
  9.6 0.7 slice_add_fusion
  10.3 1.1 maximum_bitcast_fusion.refs_5_.refs_6_.refs_4_
  11.4 18.4 %shard_map.76 = bf16[128,2048]{1,0:T(8,128)(2,1)} custom-call(bf16[3,2048,1024]{2,1,0:T(8,128)(2,1)} %refs_2_.7, bf16[3,2048,1024]{2,1,0:T(8,128)(2,1)} %refs_2_.7, bf16[3,2048,1024]{2,1,0:T(8,128)(2,1)} %refs_2_.7, f32[3,7,2048]{2,1,0:T(8,128)} %convert_bitcast_fusion.refs_4_.refs_5_.refs_3_, f32[128,2048]{1,0:T(8,128)} %maximum_bitcast_fusion.refs_5_.refs_6_.refs_4_), custom_call_target="tpu_custom_call" | custom-call | flops 81788928 | bytes 4718592 | tf_op jit(solution)/shard_map/pallas_call | solution.py:70
  29.8 16.6 %convolution_convert_fusion.3 = bf16[128,8192]{1,0:T(8,128)(2,1)} fusion(bf16[128,2048]{1,0:T(8,128)(2,1)} %shard_map.76, bf16[2048,8192]{1,0:T(8,128)(2,1)} %param.11), kind=kOutput, calls=%fused_computation.3 | convolution fusion | flops 4296015872 | bytes 36175872 | tf_op jit(solution)/shard_map/dot_general | solution.py:134
  46.4 0.0 reduce-scatter.11.cloned.1.call-update
  46.4 0.2 reduce-scatter.9.cloned.1.call-start
  46.6 35.1 %shard_map.75 = bf16[256,2048]{1,0:T(8,128)(2,1)} custom-call(bf16[3,2048,1024]{2,1,0:T(8,128)(2,1)} %refs_2_.7, bf16[3,2048,1024]{2,1,0:T(8,128)(2,1)} %refs_2_.7, bf16[3,2048,1024]{2,1,0:T(8,128)(2,1)} %refs_2_.7, bf16[3,2048,1024]{2,1,0:T(8,128)(2,1)} %refs_2_.7, f32[3,7,2048]{2,1,0:T(8,128)} %convert_bitcast_fusion.refs_4_.refs_5_.refs_3_, ...), custom_call_target="tpu_custom_call" | custom-call | flops 163577856 | bytes 6291456 | tf_op jit(solution)/shard_map/pallas_call | solution.py:70
  81.8 16.9 %convolution_convert_fusion.1 = bf16[256,8192]{1,0:T(8,128)(2,1)} fusion(bf16[256,2048]{1,0:T(8,128)(2,1)} %shard_map.75, bf16[2048,8192]{1,0:T(8,128)(2,1)} %param.11), kind=kOutput, calls=%fused_computation.1 | convolution fusion | flops 8592031744 | bytes 38797312 | tf_op jit(solution)/shard_map/dot_general | solution.py:134
  98.6 0.0 reduce-scatter.9.cloned.1.call-update
  98.7 0.3 reduce-scatter.7.cloned.1.call-start
  98.9 46.9 %shard_map.74 = bf16[384,2048]{1,0:T(8,128)(2,1)} custom-call(bf16[3,2048,1024]{2,1,0:T(8,128)(2,1)} %refs_2_.7, bf16[3,2048,1024]{2,1,0:T(8,128)(2,1)} %refs_2_.7, bf16[3,2048,1024]{2,1,0:T(8,128)(2,1)} %refs_2_.7, bf16[3,2048,1024]{2,1,0:T(8,128)(2,1)} %refs_2_.7, bf16[3,2048,1024]{2,1,0:T(8,128)(2,1)} %refs_2_.7, ...), custom_call_target="tpu_custom_call" | custom-call | flops 245366784 | bytes 7864320 | tf_op jit(solution)/shard_map/pallas_call | solution.py:70
  145.8 21.3 %convolution_convert_fusion = bf16[384,8192]{1,0:T(8,128)(2,1)} fusion(bf16[384,2048]{1,0:T(8,128)(2,1)} %shard_map.74, bf16[2048,8192]{1,0:T(8,128)(2,1)} %param.11), kind=kOutput, calls=%fused_computation | convolution fusion | flops 12888047616 | bytes 41418752 | tf_op jit(solution)/shard_map/dot_general | solution.py:134
  167.1 0.0 reduce-scatter.7.cloned.1.call-update
  167.1 0.0 reduce-scatter.5.cloned.1.call-start
  167.1 2.1 slice.9
  169.2 2.8 collective-permute-start
  172.1 4.8 %collective-permute-done.refs_0_.refs_1_ = bf16[3,2048,256]{2,1,0:T(8,128)(2,1)S(1)} collective-permute-done((bf16[3,2048,256]{2,1,0:T(8,128)(2,1)S(1)}, bf16[3,2048,256]{2,1,0:T(8,128)(2,1)S(1)}, u32[]{:S(2)}, u32[]{:S(2)}) %collective-permute-start) | collective-permute-done | bytes 3145760 | tf_op jit(solution)/shard_map/ppermute | solution.py:19
  176.9 0.0 copy-start
  176.9 1.7 copy-done
  178.6 35.1 %shard_map.73 = bf16[256,2048]{1,0:T(8,128)(2,1)} custom-call(bf16[3,2048,256]{2,1,0:T(8,128)(2,1)} %copy-done, bf16[3,2048,256]{2,1,0:T(8,128)(2,1)} %copy-done, bf16[3,2048,1024]{2,1,0:T(8,128)(2,1)} %refs_2_.7, bf16[3,2048,1024]{2,1,0:T(8,128)(2,1)} %refs_2_.7, f32[3,7,2048]{2,1,0:T(8,128)} %convert_bitcast_fusion.refs_4_.refs_5_.refs_3_, ...), custom_call_target="tpu_custom_call" | custom-call | flops 163577856 | bytes 6291456 | tf_op jit(solution)/shard_map/pallas_call | solution.py:70
  213.7 16.8 %convolution_convert_fusion.2 = bf16[256,8192]{1,0:T(8,128)(2,1)} fusion(bf16[256,2048]{1,0:T(8,128)(2,1)} %shard_map.73, bf16[2048,8192]{1,0:T(8,128)(2,1)} %param.11), kind=kOutput, calls=%fused_computation.2 | convolution fusion | flops 8592031744 | bytes 38797312 | tf_op jit(solution)/shard_map/dot_general | solution.py:134
  230.5 0.0 reduce-scatter.5.cloned.1.call-update
  230.5 0.0 reduce-scatter.11.cloned.1.call-done.refs_2_
  230.6 2.2 shard_map.77.refs_3_
  232.8 0.0 reduce-scatter.9.cloned.1.call-done.refs_2_
  232.8 4.0 %shard_map.78.refs_3_ = bf16[2048,1024]{1,0:T(8,128)(2,1)} custom-call(bf16[2048,1024]{1,0:T(8,128)(2,1)} %refs_0_.13, f32[1,2048]{1,0:T(1,128)} %bitcast.15, bf16[256,2048]{1,0:T(8,128)(2,1)} %reduce-scatter.9.cloned.1.call-done.refs_2_, bf16[2048,1024]{1,0:T(8,128)(2,1)} %shard_map.77.refs_3_), custom_call_target="tpu_custom_call", output_to_operand_aliasing={{}: (3, {})} | custom-call | flops 1048576 | bytes 3145728 | tf_op jit(solution)/shard_map/pallas_call | solution.py:109
  236.8 55.1 %reduce-scatter.7.cloned.1.call-done.refs_2_ = bf16[384,2048]{1,0:T(8,128)(2,1)} async-done(((bf16[384,8192]{1,0:T(8,128)(2,1)}), bf16[384,2048]{1,0:T(8,128)(2,1)}) %reduce-scatter.7.cloned.1.call-update) | async-done | bytes 1572880 | tf_op jit(solution)/shard_map/reduce_scatter | solution.py:135
  291.9 5.4 %shard_map.79.refs_3_ = bf16[2048,1024]{1,0:T(8,128)(2,1)} custom-call(bf16[2048,1024]{1,0:T(8,128)(2,1)} %refs_0_.13, f32[1,2048]{1,0:T(1,128)} %bitcast.16, bf16[384,2048]{1,0:T(8,128)(2,1)} %reduce-scatter.7.cloned.1.call-done.refs_2_, bf16[2048,1024]{1,0:T(8,128)(2,1)} %shard_map.78.refs_3_), custom_call_target="tpu_custom_call", output_to_operand_aliasing={{}: (3, {})} | custom-call | flops 1572864 | bytes 4718592 | tf_op jit(solution)/shard_map/pallas_call | solution.py:109
  297.3 74.1 %reduce-scatter.5.cloned.1.call-done.refs_2_ = bf16[256,2048]{1,0:T(8,128)(2,1)} async-done(((bf16[256,8192]{1,0:T(8,128)(2,1)}), bf16[256,2048]{1,0:T(8,128)(2,1)}) %reduce-scatter.5.cloned.1.call-update) | async-done | bytes 1048592 | tf_op jit(solution)/shard_map/reduce_scatter | solution.py:135
  371.4 4.0 %shard_map.80 = bf16[2048,1024]{1,0:T(8,128)(2,1)} custom-call(bf16[2048,1024]{1,0:T(8,128)(2,1)} %refs_0_.13, f32[1,2048]{1,0:T(1,128)} %bitcast.17, bf16[256,2048]{1,0:T(8,128)(2,1)} %reduce-scatter.5.cloned.1.call-done.refs_2_, bf16[2048,1024]{1,0:T(8,128)(2,1)} %shard_map.79.refs_3_), custom_call_target="tpu_custom_call", output_to_operand_aliasing={{}: (3, {})} | custom-call | flops 1048576 | bytes 3145728 | tf_op jit(solution)/shard_map/pallas_call | solution.py:109
Async XLA Ops:
  6.5 224.0 %reduce-scatter.11.cloned.1.call-start = ((), (), s32[]{:S(2)}) async-start(), calls=%async_computation.7 | async-start | bytes 2621440 | tf_op jit(solution)/shard_map/reduce_scatter | solution.py:135
  46.4 186.4 %reduce-scatter.9.cloned.1.call-start = ((), (), s32[]{:S(2)}) async-start(), calls=%async_computation.6 | async-start | bytes 5242880 | tf_op jit(solution)/shard_map/reduce_scatter | solution.py:135
  98.7 193.2 %reduce-scatter.7.cloned.1.call-start = ((), (), s32[]{:S(2)}) async-start(), calls=%async_computation.5 | async-start | bytes 7864320 | tf_op jit(solution)/shard_map/reduce_scatter | solution.py:135
  167.1 204.3 %reduce-scatter.5.cloned.1.call-start = ((), (), s32[]{:S(2)}) async-start(), calls=%async_computation.4 | async-start | bytes 5242880 | tf_op jit(solution)/shard_map/reduce_scatter | solution.py:135
  169.2 7.7 %collective-permute-start = (bf16[3,2048,256]{2,1,0:T(8,128)(2,1)S(1)}, bf16[3,2048,256]{2,1,0:T(8,128)(2,1)S(1)}, u32[]{:S(2)}, u32[]{:S(2)}) collective-permute-start(bf16[3,2048,256]{2,1,0:T(8,128)(2,1)S(1)} %slice.9), channel_id=1, source_target_pairs={{0,4},{4,8},{8,12},{12,16},{16,20},{20,24},{24,28},{1,5},{5,9},{9,... | collective-permute-start | bytes 9437192 | tf_op jit(solution)/shard_map/ppermute | solution.py:19
  176.9 1.7 copy-start
Sparse Core Ops, SparseCore 0:
  46.5 46.5 reduce-scatter.10
  98.8 79.4 reduce-scatter.8
  180.6 111.2 reduce-scatter.6
  294.0 77.2 reduce-scatter.4
